TPU v7x, 512 devices: a whole 4x8x8 slice. The times are simulated.
512 devices in a mesh: dp: 32 (over y_lo, z), tensor: 16 (over x, y_hi, core).
Axes of the slice: x: 4, y: 8 (y_hi: 2, y_lo: 4; y = y_hi * 4 + y_lo), z: 8, core: 2. Of those that a mesh axis runs over, the one named last changes fastest.
Arguments:
- emb_input: bfloat16 [4096, 16384], P('dp', 'tensor'), may hold values from -6 to 6
- cross_grad: bfloat16 [4096, 16384], P('dp', 'tensor'), may hold values from -6 to 6
- cross_weight: bfloat16 [16384, 16384], P('tensor', 'dp'), may hold values from -0.046875 to 0.046875
- direct_grad: bfloat16 [4096, 16384], P('tensor', 'dp'), may hold values from -6 to 6
- bag_ids: int32 [4096, 128, 8], P('tensor', 'dp'), may hold values from 0 to 4095
- unit_slots: int32 [32, 16], P('dp'), may hold values from 0 to 15, each once within a row
- table_rows: float32 [32, 16, 1024, 128], P('dp', 'tensor'), may hold values from -6 to 6
- adagrad_acc: float32 [32, 16, 1024], P('dp', 'tensor'), may hold values from 0.1 to 10
Outputs:
- pooled_grad: bfloat16 [4096, 16384], P('tensor', 'dp')
- new_rows: float32 [32, 16, 1024, 128], P('dp', 'tensor')
- new_acc: float32 [32, 16, 1024], P('dp', 'tensor')
Inputs may be any that keep to these rules, and one draw needn't show every extreme that they name: Each row of unit_slots names every block number once.
All inputs are finite; a program needn't handle non-finite values.
Results may differ from a plain program's by a relative error of at most 0.019.
Values may be sent and summed in bfloat16 or wider, within the bound.
A program may use at most 64 MiB of HBM per device.

v0:
```python
import math

import jax
import jax.numpy as jnp
from jax import lax
from jax.sharding import PartitionSpec as P

learn_rate = 0.5


def local(
    emb_input, cross_grad, cross_weight, direct_grad, bag_ids, unit_slots, table_rows, adagrad_acc
):
    tensor_position = lax.axis_index("tensor")
    product = (emb_input.astype(jnp.float32) * cross_grad.astype(jnp.float32)).astype(jnp.bfloat16)
    gathered = lax.all_gather(product, "dp", axis=0, tiled=True)
    summed = lax.psum_scatter(
        jnp.dot(gathered, cross_weight, preferred_element_type=jnp.float32).astype(jnp.bfloat16),
        "tensor",
        scatter_dimension=0,
        tiled=True,
    ).astype(jnp.float32)
    pooled_grad = (direct_grad.astype(jnp.float32) + summed).astype(jnp.bfloat16)
    sample_count, tables_here, bag_length = bag_ids.shape
    emb_dim = table_rows.shape[3]
    unit_rows = table_rows.shape[2]
    per_device = table_rows.shape[1]
    slot_map = unit_slots[0]
    unit_count = slot_map.shape[0]
    blocks = unit_count // tables_here
    pooled_three = pooled_grad.reshape(sample_count, tables_here, emb_dim)
    table_numbers = jnp.arange(tables_here, dtype=jnp.int32)
    owned = lax.dynamic_slice_in_dim(slot_map, tensor_position * per_device, per_device, 0)
    all_grads = lax.all_gather(pooled_three, "tensor", axis=0, tiled=True)
    all_ids = lax.all_gather(bag_ids, "tensor", axis=0, tiled=True)
    chosen = owned[:, None] // blocks == table_numbers[None, :]
    unit_grads = jnp.einsum(
        "ut,bte->ube", chosen.astype(jnp.bfloat16), all_grads, preferred_element_type=jnp.float32
    ).astype(jnp.bfloat16)
    unit_ids = jnp.sum(jnp.where(chosen[:, None, :, None], all_ids[None], 0), axis=2)
    offset = owned % blocks * unit_rows
    total_samples = unit_grads.shape[1]
    block_rows = math.gcd(total_samples, 1024)
    positions = jnp.arange(unit_rows, dtype=jnp.int32)

    def expand(running, block_index):
        row_start = block_index * block_rows
        grads_block = lax.dynamic_slice_in_dim(unit_grads, row_start, block_rows, 1)
        ids_block = (
            lax.dynamic_slice_in_dim(unit_ids, row_start, block_rows, 1) - offset[:, None, None]
        )
        counts = jnp.zeros((per_device, unit_rows, block_rows), jnp.float32)
        for bag_slot in range(bag_length):
            counts = counts + (ids_block[:, None, :, bag_slot] == positions[None, :, None]).astype(
                jnp.float32
            )
        contrib = jnp.einsum(
            "urs,use->ure",
            counts.astype(jnp.bfloat16),
            grads_block,
            preferred_element_type=jnp.float32,
        )
        return (running + contrib, None)

    row_grad, _ = lax.scan(
        expand,
        jnp.zeros((per_device, unit_rows, emb_dim), jnp.float32),
        jnp.arange(total_samples // block_rows, dtype=jnp.int32),
    )
    new_acc = adagrad_acc[0] + jnp.mean(row_grad * row_grad, axis=-1)
    new_rows = table_rows[0] - learn_rate * row_grad / jnp.sqrt(new_acc)[..., None]
    return (pooled_grad, new_rows[None], new_acc[None])


def solution(mesh):
    return jax.shard_map(
        local,
        mesh=mesh,
        in_specs=(
            P("dp", "tensor"),
            P("dp", "tensor"),
            P("tensor", "dp"),
            P("tensor", "dp"),
            P("tensor", "dp", None),
            P("dp", None),
            P("dp", "tensor", None, None),
            P("dp", "tensor", None),
        ),
        out_specs=(P("tensor", "dp"), P("dp", "tensor", None, None), P("dp", "tensor", None)),
        check_vma=False,
    )
```

profile of v0, /device:TPU:1, one launch (start us, length us, event | category | flops | bytes accessed | tf_op | source)
XLA Modules:
  0.0 424.8 jit_solution(10111367679455886127)
XLA Ops:
  7.2 0.0 copy-start
  7.2 0.0 all-gather.3.cloned.1.call-start
  7.2 1.9 multiply_convert_fusion
  9.1 0.0 all-gather.3.cloned.1.call-update
  9.1 0.0 reduce-scatter.2.cloned.1.call-start
  9.2 157.1 %all-gather.3.cloned.1.call-done = bf16[4096,1024]{1,0:T(8,128)(2,1)} async-done(((bf16[128,1024]{1,0:T(8,128)(2,1)}), bf16[4096,1024]{1,0:T(8,128)(2,1)}) %all-gather.3.cloned.1.call-update) | async-done | bytes 8388624 | tf_op jit(solution)/shard_map/all_gather | solution.py:16
  166.3 0.0 copy-done
  166.3 9.4 %convolution_convert_fusion = bf16[4096,512]{1,0:T(8,128)(2,1)} fusion(bf16[4096,1024]{1,0:T(8,128)(2,1)} %all-gather.3.cloned.1.call-done, bf16[1024,512]{1,0:T(8,128)(2,1)S(1)} %copy-done), kind=kOutput, calls=%fused_computation.17 | convolution fusion | flops 4297064448 | bytes 13631488 | tf_op jit(solution)/shard_map/dot_general | solution.py:18
  175.8 0.0 copy-start.3
  175.8 0.0 copy-start.6
  175.8 0.0 copy-start.4
  175.8 0.0 reduce-scatter.2.cloned.1.call-update
  175.8 0.0 all-gather.5.cloned.1.call-start
  175.8 125.6 %reduce-scatter.2.cloned.1.call-done = bf16[256,512]{1,0:T(8,128)(2,1)} async-done(((bf16[4096,512]{1,0:T(8,128)(2,1)}), bf16[256,512]{1,0:T(8,128)(2,1)}) %reduce-scatter.2.cloned.1.call-update) | async-done | bytes 262160 | tf_op jit(solution)/shard_map/reduce_scatter | solution.py:17
  301.5 0.0 copy-done.3
  301.5 1.0 add_convert_fusion.6
  302.5 0.0 copy-start.1
  302.5 0.8 reshape.246
  303.3 0.0 all-gather.5.cloned.1.call-update
  303.3 0.0 copy-done.6
  303.3 0.7 fusion.13
  308.8 0.0 copy-done.4
  308.8 32.8 %all_gather.10 = s32[4096,4,8]{0,2,1:T(8,128)S(1)} all-gather(s32[256,4,8]{0,2,1:T(8,128)S(1)} %copy-done.4), channel_id=1, replica_groups=mesh['dp'=32,'tensor'=16] {'tensor'}, dimensions={0}, use_global_device_ids=true | all-gather | bytes 557056 | tf_op jit(solution)/shard_map/all_gather | solution.py:35
  341.5 0.1 select_reduce_fusion
  341.7 48.5 %all-gather.5.cloned.1.call-done = bf16[4096,4,128]{2,1,0:T(4,128)(2,1)} async-done(((bf16[256,4,128]{2,1,0:T(4,128)(2,1)}), bf16[4096,4,128]{2,1,0:T(4,128)(2,1)}) %all-gather.5.cloned.1.call-update) | async-done | bytes 4194320 | tf_op jit(solution)/shard_map/all_gather | solution.py:34
  390.2 4.5 %fusion.8 = f32[1,524288]{1,0:T(1,128)S(1)} fusion(bf16[4096,4,128]{2,1,0:T(4,128)(2,1)} %all-gather.5.cloned.1.call-done, s32[]{:T(128)} %bitcast.1), kind=kOutput, calls=%fused_computation.18 | convolution fusion | flops 4194308 | bytes 6291460
  394.7 0.0 copy-done.1
  394.7 0.1 convert_bitcast_fusion
  394.8 0.0 copy-start.5
  394.8 0.0 copy-start.2
  394.8 21.5 %while.12 = (s32[]{:T(128)}, f32[1,1024,128]{2,1,0:T(8,128)S(1)}, s32[4]{0:T(128)S(1)}, s32[1,4096,8]{1,2,0:T(8,128)S(1)}, s32[1]{0:T(128)}, /*index=5*/bf16[1,4...) while((s32[]{:T(128)}, f32[1,1024,128]{2,1,0:T(8,128)S(1)}, ...), condition=%wide.region_3.4_spmd.clone.clone, body=%wide.region_2.3_spmd.clone.clone.sunk | while | flops 293871616 | bytes 1474749 | solution.py:65
  394.9 0.6 dynamic_slice.34
  396.2 4.1 fusion.21
  400.2 0.6 dynamic_slice.34
  401.5 4.1 fusion.21
  405.6 0.6 dynamic_slice.34
  406.9 4.1 fusion.21
  411.0 0.6 dynamic_slice.34
  412.3 4.1 fusion.21
  416.4 0.2 multiply_reduce_fusion
  416.6 0.0 copy-done.5
  416.6 0.6 add.91
  417.2 0.0 copy-done.2
  417.2 1.0 fusion.10
  (12 shorter events, 0.2 us)
Async XLA Ops:
  7.2 159.2 %copy-start = (bf16[1024,512]{1,0:T(8,128)(2,1)S(1)}, bf16[1024,512]{1,0:T(8,128)(2,1)}, u32[]{:S(2)}) copy-start(bf16[1024,512]{1,0:T(8,128)(2,1)} %param.12) | copy-start | bytes 3145732
  7.2 159.1 %all-gather.3.cloned.1.call-start = ((), (), s32[]{:S(2)}) async-start(), calls=%async_computation.1 | async-start | bytes 8650752 | tf_op jit(solution)/shard_map/all_gather | solution.py:16
  9.1 292.3 %reduce-scatter.2.cloned.1.call-start = ((), (), s32[]{:S(2)}) async-start(), calls=%async_computation.2 | async-start | bytes 4456448 | tf_op jit(solution)/shard_map/reduce_scatter | solution.py:17
  175.8 125.7 %copy-start.3 = (bf16[256,512]{1,0:T(8,128)(2,1)S(1)}, bf16[256,512]{1,0:T(8,128)(2,1)}, u32[]{:S(2)}) copy-start(bf16[256,512]{1,0:T(8,128)(2,1)} %param.13) | copy-start | bytes 786436
  175.8 127.6 %copy-start.6 = (s32[1,16]{1,0:T(1,128)S(1)}, s32[1,16]{1,0:T(1,128)}, u32[]{:S(2)}) copy-start(s32[1,16]{1,0:T(1,128)} %param.15) | copy-start | bytes 196
  175.8 133.0 %copy-start.4 = (s32[256,4,8]{0,2,1:T(8,128)S(1)}, s32[256,4,8]{0,2,1:T(8,128)}, u32[]{:S(2)}) copy-start(s32[256,4,8]{0,2,1:T(8,128)} %param.14) | copy-start | bytes 98308
  175.8 214.4 %all-gather.5.cloned.1.call-start = ((), (), s32[]{:S(2)}) async-start(), calls=%async_computation.3 | async-start | bytes 4456448 | tf_op jit(solution)/shard_map/all_gather | solution.py:34
  302.5 92.2 %copy-start.1 = (bf16[256,512]{1,0:T(8,128)(2,1)}, bf16[256,512]{1,0:T(8,128)(2,1)S(1)}, u32[]{:S(2)}) copy-start(bf16[256,512]{1,0:T(8,128)(2,1)S(1)} %add_convert_fusion.6) | copy-start | bytes 786436
  394.8 21.8 %copy-start.5 = (f32[1,1,1024]{2,1,0:T(1,128)S(1)}, f32[1,1,1024]{2,1,0:T(1,128)}, u32[]{:S(2)}) copy-start(f32[1,1,1024]{2,1,0:T(1,128)} %param.17) | copy-start | bytes 12292
  394.8 22.4 %copy-start.2 = (f32[1,1,1024,128]{3,2,1,0:T(8,128)S(1)}, f32[1,1,1024,128]{3,2,1,0:T(8,128)}, u32[]{:S(2)}) copy-start(f32[1,1,1024,128]{3,2,1,0:T(8,128)} %param.16) | copy-start | bytes 1572868
Sparse Core Ops, SparseCore 0:
  10.7 155.6 all-gather.2
  175.9 125.5 reduce-scatter.1
  305.8 84.3 all-gather.4
where the time goes:
time: 425 us
  waiting for transfers between devices  331 us (78%)
  blocking collectives  32.8 us (8%)
  matrix products  30.2 us (7%)
  between operations  18.6 us (4%)
  other arithmetic  5.65 us (1%)
    all_gather x1, waiting for transfers between devices, local(): gathered = lax.all_gather(product, 'dp', axis=0, tiled=True)  157 us
    reduce_scatter x1, waiting for transfers between devices, local(): lax.psum_scatter(jnp.dot(gathered, cross_weight, preferred_element_type=j...  126 us
    all_gather x1, waiting for transfers between devices, local(): all_grads = lax.all_gather(pooled_three, 'tensor', axis=0, tiled=True)  48.5 us
    all_gather x1, blocking collectives, local(): all_ids = lax.all_gather(bag_ids, 'tensor', axis=0, tiled=True)  32.8 us
    dot_general x4, matrix products, expand(): jnp.einsum('urs,use->ure', counts.astype(jnp.bfloat16), grads_block, pref...  16.3 us
    dot_general x1, matrix products, local(): jnp.dot(gathered, cross_weight, preferred_element_type=jnp.float32)  9.43 us
  transfers between devices with their start and end apart: 3, of which 3 were waited for; matrix products, arithmetic and copies ran while one was open for 0% of the time, Pallas kernels for 0%

commit v1 on v0

v1 whole, which is shorter than its diff:
```python
import jax
import jax.numpy as jnp
from jax import lax
from jax.experimental import pallas as pl
from jax.experimental.pallas import tpu as pltpu
from jax.sharding import PartitionSpec as P

learn_rate = 0.5
F32 = jnp.float32
BF16 = jnp.bfloat16


def kernel(
    emb_ref, cross_ref, weight_ref, direct_ref, ids_ref, slots_ref, rows_ref, acc_ref,
    pooled_ref, new_rows_ref, new_acc_ref,
    factors, blocks, weights, direct, rows, acc_in, acc_wide,
    partial, core_in, summed, from_far, from_minus, from_plus, reduced,
    held, stage, table_grads, ids_stage, ids_all, counts, row_grad, acc_out,
    local_sem, up_send, up_recv, down_send, down_recv, pair_send, pair_recv,
    core_send, core_recv, x_send, far_recv, minus_recv, plus_recv, own_recv,
    final_send, final_recv, half_send, half_recv, table_send, table_recv, ids_send, ids_recv,
):
    dp = lax.axis_index("dp")
    me = lax.axis_index("tensor")
    y, z = dp // 8, dp % 8
    x, h, c = me // 4, (me // 2) % 2, me % 2
    y1 = y + 1 - 2 * (y % 2)
    y2 = (y + 2) % 4
    active = x % 2 == y % 2
    odd = z % 2

    def tensor_of(xx, hh, cc):
        return (xx * 2 + hh) * 2 + cc

    def remote(src, dst, send, recv, to_dp, to_tensor):
        return pltpu.make_async_remote_copy(
            src_ref=src, dst_ref=dst, send_sem=send, recv_sem=recv,
            device_id=(to_dp, to_tensor), device_id_type=pl.DeviceIdType.MESH,
        )

    def arrived(dst, recv, send):
        remote(dst, dst, send, recv, dp, (me + 1) % 16).wait_recv()

    def sent(src, send, recv):
        remote(src, src, send, recv, dp, (me + 1) % 16).wait_send()

    def at_dp(yy, zz):
        return yy * 8 + zz

    barrier = pltpu.get_barrier_semaphore()

    def greet(to_dp, to_tensor):
        pl.semaphore_signal(
            barrier, inc=1, device_id=(to_dp, to_tensor), device_id_type=pl.DeviceIdType.MESH
        )

    up, down = (z + 1) % 8, (z + 7) % 8
    greet(at_dp(y, up), me)
    greet(at_dp(y, down), me)
    greet(at_dp(y2, z), me)
    greet(at_dp(y1, z), me)
    greet(at_dp(y1, z), tensor_of(x, 1 - h, c))

    @pl.loop(1, 16)
    def _(i):
        greet(dp, (me + i) % 16)

    loads = [
        pltpu.make_async_copy(emb_ref, factors.at[0], local_sem.at[0]),
        pltpu.make_async_copy(cross_ref, factors.at[1], local_sem.at[1]),
        pltpu.make_async_copy(weight_ref, weights.at[0], local_sem.at[2]),
        pltpu.make_async_copy(acc_ref, acc_in, local_sem.at[3]),
        pltpu.make_async_copy(direct_ref, direct, local_sem.at[4]),
        pltpu.make_async_copy(rows_ref, rows, local_sem.at[5]),
    ]
    for load in loads:
        load.start()
    loads[0].wait()
    loads[1].wait()

    def place(origin, slot, first=0, count=128):
        start = pl.multiple_of(slot * 256 + (origin % 2) * 128 + first, 64)
        return blocks.at[origin // 2, pl.ds(start, count), :]

    own = place(z, 0)
    own[...] = (factors[0].astype(F32) * factors[1].astype(F32)).astype(BF16)

    pl.semaphore_wait(barrier, 20)

    def ring_up(step, slot):
        origin = (z + 9 - step) % 8
        ref = place(origin, slot, 0, 64 if step == 4 else 128)
        return remote(
            ref, ref, up_send.at[step - 1, slot], up_recv.at[step - 1, slot], at_dp(y, up), me
        )

    def ring_down(step, slot):
        origin = (z + step - 1) % 8
        ref = place(origin, slot, 64, 64) if step == 4 else place(origin, slot)
        return remote(
            ref, ref, down_send.at[step - 1, slot], down_recv.at[step - 1, slot], at_dp(y, down), me
        )

    def ring_start(step, slot):
        ring_up(step, slot).start()
        ring_down(step, slot).start()

    def ring_wait(step, slot):
        low = place((z + 8 - step) % 8, slot, 0, 64 if step == 4 else 128)
        arrived(low, up_recv.at[step - 1, slot], up_send.at[step - 1, slot])
        high_origin = (z + step) % 8
        high = place(high_origin, slot, 64, 64) if step == 4 else place(high_origin, slot)
        arrived(high, down_recv.at[step - 1, slot], down_send.at[step - 1, slot])

    ring_start(1, 0)
    to_pair = remote(
        own, place(z, 1), pair_send.at[0], pair_recv.at[0], at_dp(y2, z), me
    )
    to_pair.start()
    to_side = remote(
        weight_ref, weights.at[1], pair_send.at[1], pair_recv.at[1], at_dp(y1, z), me
    )
    to_side.start()

    def ids_copy(i):
        to = (me + i) % 16
        return remote(
            ids_stage.at[i], ids_all.at[me], ids_send.at[i], ids_recv.at[me], dp, to
        )

    def ids_of(owner):
        table = slots_ref[0, owner]
        value = ids_ref[0]
        for number in range(1, 4):
            value = jnp.where(table == number, ids_ref[number], value)
        return value

    ids_all[me] = ids_of(me)

    @pl.loop(1, 16)
    def _(i):
        ids_stage[i] = ids_of((me + i) % 16)
        ids_copy(i).start()

    loads[3].wait()
    acc_wide[...] = jnp.broadcast_to(acc_in[...], (128, 1024)).T

    first_row = slots_ref[1, me]

    def count(low, high):
        @pl.loop(low, high)
        def _(i):
            source = (me + i) % 16

            @pl.when(i != 0)
            def _():
                arrived(ids_all.at[source], ids_recv.at[source], ids_send.at[i])

            ids = ids_all[source]

            @pl.loop(0, 16)
            def _(r):
                base = pl.multiple_of(r * 64, 64)
                positions = lax.broadcasted_iota(jnp.int32, (64, 256), 0) + (base + first_row)
                total = jnp.zeros((64, 256), F32)
                for bag in range(8):
                    total = total + jnp.where(positions == ids[bag : bag + 1, :], 1.0, 0.0)
                counts[source, pl.ds(base, 64), :] = total.astype(BF16)

    m0 = z // 2
    pair_of = [m0, (m0 + 3 + 2 * odd) % 4, (m0 + 5 - 2 * odd) % 4, (m0 + 2) % 4]
    apart = (2 * h + c - m0 + 4) % 4
    my_step = jnp.where(
        apart == 0, 0, jnp.where(apart == 2, 3, jnp.where(apart == 1, 2 - odd, 1 + odd))
    )

    dest_x = (y + 2 * c) % 4
    ahead = (dest_x - x + 4) % 4

    def multiply(step, side):
        unit = 2 * step + side
        block = pair_of[step]

        @pl.loop(0, 2)
        def _(n):
            cols = pl.ds(pl.multiple_of(n * 256, 256), 256)
            part = jnp.dot(
                blocks[block], weights[side, :, cols], preferred_element_type=F32
            ).astype(BF16)
            partial[unit, 0, :, cols] = part[:256]
            partial[unit, 1, :, cols] = part[256:]

        remote(
            partial.at[unit, 1 - c], core_in.at[unit], core_send.at[unit], core_recv.at[unit],
            dp, tensor_of(x, h, 1 - c),
        ).start()

    def by_rows(body):
        @pl.loop(0, 4)
        def _(r):
            body(pl.ds(pl.multiple_of(r * 64, 64), 64))

    def send_on(step, side):
        unit = 2 * step + side
        to = tensor_of(dest_x, h, pair_of[step] % 2)

        @pl.when(ahead == 1)
        def _():
            remote(
                summed.at[0, unit], from_minus.at[unit], x_send.at[unit], minus_recv.at[unit], dp, to
            ).start()

        @pl.when(ahead == 3)
        def _():
            remote(
                summed.at[0, unit], from_plus.at[unit], x_send.at[unit], plus_recv.at[unit], dp, to
            ).start()

    def combine(step, side):
        unit = 2 * step + side
        arrived(core_in.at[unit], core_recv.at[unit], core_send.at[unit])

        def body(part):
            summed[0, unit, part, :] = (
                partial[unit, c, part, :].astype(F32) + core_in[unit, part, :].astype(F32)
            ).astype(BF16)

        by_rows(body)

        @pl.when((ahead == 0) & (c != pair_of[step] % 2))
        def _():
            remote(
                summed.at[0, unit], summed.at[1, unit], x_send.at[unit], own_recv.at[unit],
                dp, tensor_of(x, h, 1 - c),
            ).start()

        @pl.when(ahead == 2)
        def _():
            relay = (x + (1 if side == 0 else 3)) % 4
            remote(
                summed.at[0, unit], from_far.at[unit], x_send.at[unit], far_recv.at[unit],
                dp, tensor_of(relay, h, c),
            ).start()

        @pl.when(ahead == (3 if side == 0 else 1))
        def _():
            send_on(step, side)

    def relay_on(step, side):
        unit = 2 * step + side

        @pl.when(ahead == (1 if side == 0 else 3))
        def _():
            arrived(from_far.at[unit], far_recv.at[unit], x_send.at[unit])

            def body(part):
                summed[0, unit, part, :] = (
                    summed[0, unit, part, :].astype(F32) + from_far[unit, part, :].astype(F32)
                ).astype(BF16)

            by_rows(body)
            send_on(step, side)

    other_core = jnp.where((x == y) == (c == 0), 0, 1)

    def reduces(step):
        return active & (c == pair_of[step] % 2)

    def final_remote(step, side):
        unit = 2 * step + side
        home = pair_of[step] // 2
        here = 1 - (home - h) * (home - h)
        return remote(
            reduced.at[unit], reduced.at[9 - here], final_send.at[unit], final_recv.at[1 - here],
            at_dp(y1 if side else y, z), tensor_of(x, home, c),
        )

    def stays(step, side):
        return (pair_of[step] // 2 == h) if side == 0 else False

    def reduce_x(step, side):
        unit = 2 * step + side

        @pl.when(reduces(step))
        def _():
            @pl.when(other_core == 1)
            def _():
                arrived(summed.at[1, unit], own_recv.at[unit], x_send.at[unit])

            arrived(from_minus.at[unit], minus_recv.at[unit], x_send.at[unit])
            arrived(from_plus.at[unit], plus_recv.at[unit], x_send.at[unit])
            if side == 0:
                home = pair_of[step] // 2
                target = jnp.where(home == h, 8, unit)
            else:
                target = unit

            def body(part):
                reduced[target, part, :] = (
                    summed[other_core, unit, part, :].astype(F32)
                    + from_minus[unit, part, :].astype(F32)
                    + from_plus[unit, part, :].astype(F32)
                ).astype(BF16)

            by_rows(body)
            if side == 0:

                @pl.when(pair_of[step] // 2 != h)
                def _():
                    final_remote(step, side).start()

            else:
                final_remote(step, side).start()

    def table_copy(half, i):
        spot = ((2 * x + c) + i) % 8
        to = tensor_of(spot // 2, h, spot % 2)
        source = tensor_of(x, (h + half) % 2, c)
        return remote(
            stage.at[half, i], table_grads.at[source], table_send.at[half, i],
            table_recv.at[source], dp, to,
        )

    def send_tables(half):
        source = tensor_of(x, (h + half) % 2, c)

        def chosen(owner):
            table = slots_ref[0, owner]
            value = held[half, :, 0:128]
            for number in range(1, 4):
                columns = held[half, :, 128 * number : 128 * (number + 1)]
                value = jnp.where(table == number, columns, value)
            return value

        @pl.loop(1, 8)
        def _(i):
            spot = ((2 * x + c) + i) % 8
            stage[half, i] = chosen(tensor_of(spot // 2, h, spot % 2))
            table_copy(half, i).start()

        table_grads[source] = chosen(me)

    to_half = remote(
        held.at[0], held.at[1], half_send.at[0], half_recv.at[0], dp, tensor_of(x, 1 - h, c)
    )
    write_pooled = pltpu.make_async_copy(held.at[0], pooled_ref, local_sem.at[6])

    def finish_pooled():
        @pl.when(jnp.logical_not(active))
        def _():
            arrived(reduced.at[8], final_recv.at[0], final_send.at[0])

        arrived(reduced.at[9], final_recv.at[1], final_send.at[0])

        def body(part):
            held[0, part, :] = (
                direct[part, :].astype(F32)
                + (reduced[8, part, :].astype(F32) + reduced[9, part, :].astype(F32))
            ).astype(BF16)

        by_rows(body)
        to_half.start()
        write_pooled.start()
        send_tables(0)

    def finish_other():
        arrived(held.at[1], half_recv.at[0], half_send.at[0])
        send_tables(1)

    def scatter(step):
        @pl.loop(0, 4)
        def _(xx):
            source = 4 * xx + pair_of[step]

            @pl.when((xx != x) | (pair_of[step] % 2 != c))
            def _():
                arrived(table_grads.at[source], table_recv.at[source], table_send.at[0, 1])

            row_grad[...] += jnp.dot(
                counts[source], table_grads[source], preferred_element_type=F32
            )

    row_grad[...] = jnp.zeros_like(row_grad)
    arrived(place(z, 1), pair_recv.at[0], pair_send.at[0])
    ring_start(1, 1)
    loads[2].wait()
    ring_wait(1, 0)
    ring_start(2, 0)
    count(0, 3)
    ring_wait(1, 1)
    ring_start(2, 1)
    multiply(0, 0)
    count(3, 6)
    ring_wait(2, 0)
    ring_start(3, 0)
    combine(0, 0)
    count(6, 9)
    ring_wait(2, 1)
    ring_start(3, 1)
    multiply(1, 0)
    relay_on(0, 0)
    count(9, 12)
    combine(1, 0)
    ring_wait(3, 0)
    ring_start(4, 0)
    reduce_x(0, 0)
    relay_on(1, 0)
    count(12, 16)
    loads[4].wait()
    loads[5].wait()
    ring_wait(3, 1)
    ring_start(4, 1)
    arrived(weights.at[1], pair_recv.at[1], pair_send.at[1])
    multiply(0, 1)
    multiply(1, 1)
    combine(0, 1)
    multiply(2, 0)
    combine(1, 1)
    multiply(2, 1)
    relay_on(0, 1)
    relay_on(1, 1)
    combine(2, 0)
    combine(2, 1)
    ring_wait(4, 0)
    ring_wait(4, 1)
    multiply(3, 0)
    multiply(3, 1)
    relay_on(2, 0)
    relay_on(2, 1)
    combine(3, 0)
    combine(3, 1)
    reduce_x(1, 0)
    reduce_x(0, 1)
    reduce_x(1, 1)
    relay_on(3, 0)
    reduce_x(2, 0)
    relay_on(3, 1)
    reduce_x(2, 1)

    @pl.when(my_step != 3)
    def _():
        finish_pooled()

    @pl.when(my_step != 0)
    def _():
        finish_other()

    reduce_x(3, 0)
    reduce_x(3, 1)

    @pl.when(my_step == 3)
    def _():
        finish_pooled()

    @pl.when(my_step == 0)
    def _():
        finish_other()

    scatter(0)
    scatter(1)
    scatter(2)
    scatter(3)

    new_acc = acc_wide[...] + jnp.mean(row_grad[...] * row_grad[...], axis=-1, keepdims=True)
    rows[...] = rows[...] - learn_rate * row_grad[...] / jnp.sqrt(new_acc)
    acc_out[...] = new_acc.T[0:1, :]
    write_rows = pltpu.make_async_copy(rows, new_rows_ref, local_sem.at[7])
    write_acc = pltpu.make_async_copy(acc_out, new_acc_ref, local_sem.at[8])
    write_rows.start()
    write_acc.start()

    for step in range(1, 5):
        for slot in range(2):
            ring_up(step, slot).wait_send()
            ring_down(step, slot).wait_send()
    to_pair.wait_send()
    to_side.wait_send()

    @pl.loop(1, 16)
    def _(i):
        ids_copy(i).wait_send()

    for step in range(4):
        for side in range(2):
            unit = 2 * step + side
            sent(partial.at[unit, 0], core_send.at[unit], core_recv.at[unit])

            @pl.when((ahead != 0) | (c != pair_of[step] % 2))
            def _():
                sent(summed.at[0, unit], x_send.at[unit], own_recv.at[unit])

            away = reduces(step)
            if side == 0:
                away = away & (pair_of[step] // 2 != h)

            @pl.when(away)
            def _():
                sent(reduced.at[unit], final_send.at[unit], final_recv.at[0])

    to_half.wait_send()

    @pl.loop(1, 8)
    def _(i):
        table_copy(0, i).wait_send()
        table_copy(1, i).wait_send()

    write_pooled.wait()
    write_rows.wait()
    write_acc.wait()


def local(
    emb_input, cross_grad, cross_weight, direct_grad, bag_ids, unit_slots, table_rows, adagrad_acc
):
    anywhere = pl.BlockSpec(memory_space=pl.ANY)
    dma = pltpu.SemaphoreType.DMA
    pooled, new_rows, new_acc = pl.pallas_call(
        kernel,
        out_shape=(
            jax.ShapeDtypeStruct((256, 512), BF16),
            jax.ShapeDtypeStruct((1024, 128), F32),
            jax.ShapeDtypeStruct((1, 1024), F32),
        ),
        in_specs=[anywhere] * 4
        + [pl.BlockSpec(memory_space=pltpu.VMEM), pl.BlockSpec(memory_space=pltpu.SMEM)]
        + [anywhere] * 2,
        out_specs=(anywhere,) * 3,
        scratch_shapes=[
            pltpu.VMEM((2, 128, 1024), BF16),
            pltpu.VMEM((4, 512, 1024), BF16),
            pltpu.VMEM((2, 1024, 512), BF16),
            pltpu.VMEM((256, 512), BF16),
            pltpu.VMEM((1024, 128), F32),
            pltpu.VMEM((1, 1024), F32),
            pltpu.VMEM((1024, 128), F32),
            pltpu.VMEM((8, 2, 256, 512), BF16),
            pltpu.VMEM((8, 256, 512), BF16),
            pltpu.VMEM((2, 8, 256, 512), BF16),
            pltpu.VMEM((8, 256, 512), BF16),
            pltpu.VMEM((8, 256, 512), BF16),
            pltpu.VMEM((8, 256, 512), BF16),
            pltpu.VMEM((10, 256, 512), BF16),
            pltpu.VMEM((2, 256, 512), BF16),
            pltpu.VMEM((2, 8, 256, 128), BF16),
            pltpu.VMEM((16, 256, 128), BF16),
            pltpu.VMEM((16, 8, 256), jnp.int32),
            pltpu.VMEM((16, 8, 256), jnp.int32),
            pltpu.VMEM((16, 1024, 256), BF16),
            pltpu.VMEM((1024, 128), F32),
            pltpu.VMEM((1, 1024), F32),
            dma((9,)),
            dma((4, 2)),
            dma((4, 2)),
            dma((4, 2)),
            dma((4, 2)),
            dma((2,)),
            dma((2,)),
            dma((8,)),
            dma((8,)),
            dma((8,)),
            dma((8,)),
            dma((8,)),
            dma((8,)),
            dma((8,)),
            dma((8,)),
            dma((2,)),
            dma((1,)),
            dma((1,)),
            dma((2, 8)),
            dma((16,)),
            dma((16,)),
            dma((16,)),
        ],
        compiler_params=pltpu.CompilerParams(
            collective_id=1, has_side_effects=True, vmem_limit_bytes=56 * 2**20
        ),
        cost_estimate=pl.CostEstimate(
            flops=5_400_000_000, bytes_accessed=4_000_000, transcendentals=1024
        ),
    )(
        emb_input,
        cross_grad,
        cross_weight,
        direct_grad,
        jnp.transpose(bag_ids, (1, 2, 0)),
        jnp.concatenate([unit_slots // 4, unit_slots % 4 * 1024]),
        table_rows[0, 0],
        adagrad_acc[0],
    )
    return (pooled, new_rows[None, None], new_acc[None])


def solution(mesh):
    return jax.shard_map(
        local,
        mesh=mesh,
        in_specs=(
            P("dp", "tensor"),
            P("dp", "tensor"),
            P("tensor", "dp"),
            P("tensor", "dp"),
            P("tensor", "dp", None),
            P("dp", None),
            P("dp", "tensor", None, None),
            P("dp", "tensor", None),
        ),
        out_specs=(P("tensor", "dp"), P("dp", "tensor", None, None), P("dp", "tensor", None)),
        check_vma=False,
    )
```

time: 425 us -> 143 us (0.34)
  the two profiles are of different devices: /device:TPU:1 before, /device:TPU:73 now
where the time goes in v1:
time: 143 us
  Pallas kernels  138 us (97%)
  local copies, waits for them, and re-layouts  3.77 us (3%)
    pallas_call x1, Pallas kernels, local(): pl.pallas_call(kernel, out_shape=(jax.ShapeDtypeStruct((256, 512), BF16),...  138 us
    unnamed x9, local copies, waits for them, and re-layouts  3.77 us

profile of v1, /device:TPU:73, one launch (start us, length us, event | category | flops | bytes accessed | tf_op | source)
XLA Modules:
  0.0 143.1 jit_solution(12458174029830927740)
XLA Ops:
  0.6 0.0 copy-start.2
  0.6 0.6 copy-done.2
  1.3 0.6 pad_add_fusion.slots_ref
  1.9 138.1 %shard_map.103 = (bf16[256,512]{1,0:T(8,128)(2,1)}, f32[1024,128]{1,0:T(8,128)}, f32[1,1024]{1,0:T(1,128)}) custom-call(bf16[128,1024]{1,0:T(8,128)(2,1)} %emb_ref.1, bf16[128,1024]{1,0:T(8,128)(2,1)} %cross_ref.1, bf16[1024,512]{1,0:T(8,128)(2,1)} %weight_ref.1, bf16[256,512]{1,0:T(8,128)(2,1)} %direct_ref.1, s32[4,8,256]{2,1,0:T(8,128)} %bitcast.8, ...), custom_call_target="tpu_custom_call" | custom-call | flops 5400000000 | bytes 4000000 | tf_op jit(solution)/shard_map/pallas_call | solution.py:517
  140.0 0.0 copy-start
  140.0 1.7 %copy.14 = bf16[256,512]{1,0:T(8,128)(2,1)} copy(bf16[256,512]{1,0:T(8,128)(2,1)} %get-tuple-element.14) | data formatting | bytes 524288
  141.7 0.0 copy-done
  141.7 0.0 copy-start.1
  141.7 0.8 copy.15
  142.5 0.0 copy-done.1
  142.5 0.6 copy.16
  (1 shorter events, 0.0 us)
Async XLA Ops:
  0.6 0.7 copy-start.2
  140.0 1.7 %copy-start = (f32[1024,128]{1,0:T(8,128)S(1)}, f32[1024,128]{1,0:T(8,128)}, u32[]{:S(2)}) copy-start(f32[1024,128]{1,0:T(8,128)} %get-tuple-element.7) | copy-start | bytes 1572868
  141.7 0.8 copy-start.1

commit v2 on v1

--- a/solution.py
+++ b/solution.py
@@ -11,14 +11,14 @@
 
 
 def kernel(
-    emb_ref, cross_ref, weight_ref, direct_ref, ids_ref, slots_ref, rows_ref, acc_ref,
-    pooled_ref, new_rows_ref, new_acc_ref,
-    factors, blocks, weights, direct, rows, acc_in, acc_wide,
+    emb_ref, cross_ref, weight_ref, direct_ref, ids_ref, slots_ref,
+    pooled_ref, row_grad_ref,
+    factors, blocks, weights, direct,
     partial, core_in, summed, from_far, from_minus, from_plus, reduced,
-    held, stage, table_grads, ids_stage, ids_all, counts, row_grad, acc_out,
+    held, stage, table_grads, ids_stage, ids_all, packed, counts, row_grad,
     local_sem, up_send, up_recv, down_send, down_recv, pair_send, pair_recv,
     core_send, core_recv, x_send, far_recv, minus_recv, plus_recv, own_recv,
-    final_send, final_recv, half_send, half_recv, table_send, table_recv, ids_send, ids_recv,
+    final_send, final_recv, table_send, table_recv, ids_send, ids_recv,
 ):
     dp = lax.axis_index("dp")
     me = lax.axis_index("tensor")
@@ -69,9 +69,7 @@
         pltpu.make_async_copy(emb_ref, factors.at[0], local_sem.at[0]),
         pltpu.make_async_copy(cross_ref, factors.at[1], local_sem.at[1]),
         pltpu.make_async_copy(weight_ref, weights.at[0], local_sem.at[2]),
-        pltpu.make_async_copy(acc_ref, acc_in, local_sem.at[3]),
-        pltpu.make_async_copy(direct_ref, direct, local_sem.at[4]),
-        pltpu.make_async_copy(rows_ref, rows, local_sem.at[5]),
+        pltpu.make_async_copy(direct_ref, direct.at[0], local_sem.at[3]),
     ]
     for load in loads:
         load.start()
@@ -120,7 +118,10 @@
     to_side = remote(
         weight_ref, weights.at[1], pair_send.at[1], pair_recv.at[1], at_dp(y1, z), me
     )
-    to_side.start()
+
+    to_other = remote(
+        direct_ref, direct.at[1], pair_send.at[2], pair_recv.at[2], dp, tensor_of(x, 1 - h, c)
+    )
 
     def ids_copy(i):
         to = (me + i) % 16
@@ -129,10 +130,10 @@
         )
 
     def ids_of(owner):
-        table = slots_ref[0, owner]
+        slot = slots_ref[0, owner]
         value = ids_ref[0]
         for number in range(1, 4):
-            value = jnp.where(table == number, ids_ref[number], value)
+            value = jnp.where(slot >= 4 * number, ids_ref[number], value)
         return value
 
     ids_all[me] = ids_of(me)
@@ -142,10 +143,7 @@
         ids_stage[i] = ids_of((me + i) % 16)
         ids_copy(i).start()
 
-    loads[3].wait()
-    acc_wide[...] = jnp.broadcast_to(acc_in[...], (128, 1024)).T
-
-    first_row = slots_ref[1, me]
+    first_row = (slots_ref[0, me] & 3) * 1024
 
     def count(low, high):
         @pl.loop(low, high)
@@ -156,24 +154,37 @@
             def _():
                 arrived(ids_all.at[source], ids_recv.at[source], ids_send.at[i])
 
-            ids = ids_all[source]
-
-            @pl.loop(0, 16)
+            ids = ids_all[source] - first_row
+            digit = jnp.where((ids & 1) != 0, 16, 1) * jnp.where((ids & 2) != 0, 256, 1)
+            digit = digit * jnp.where((ids & 4) != 0, 65536, 1)
+            word = lax.shift_right_arithmetic(ids, 3)
+            numbers = lax.broadcasted_iota(jnp.int32, (128, 256), 0)
+            total = jnp.zeros((128, 256), jnp.int32)
+            for bag in range(8):
+                total = total + jnp.where(
+                    numbers == word[bag : bag + 1, :], digit[bag : bag + 1, :], 0
+                )
+            packed[...] = total
+            shifts = 4 * lax.broadcasted_iota(jnp.int32, (8, 256), 0)
+            cols = pl.ds(pl.multiple_of((source // 4) * 256, 256), 256)
+
+            @pl.loop(0, 8)
             def _(r):
-                base = pl.multiple_of(r * 64, 64)
-                positions = lax.broadcasted_iota(jnp.int32, (64, 256), 0) + (base + first_row)
-                total = jnp.zeros((64, 256), F32)
-                for bag in range(8):
-                    total = total + jnp.where(positions == ids[bag : bag + 1, :], 1.0, 0.0)
-                counts[source, pl.ds(base, 64), :] = total.astype(BF16)
+                words = packed[pl.ds(pl.multiple_of(r * 16, 16), 16), :]
+                for n in range(8):
+                    both = [
+                        lax.shift_right_logical(
+                            jnp.broadcast_to(words[k : k + 1, :], (8, 256)), shifts
+                        )
+                        & 15
+                        for k in (2 * n, 2 * n + 1)
+                    ]
+                    counts[
+                        source % 4, pl.ds(pl.multiple_of(r * 128 + n * 16, 16), 16), cols
+                    ] = jnp.concatenate(both).astype(F32).astype(BF16)
 
     m0 = z // 2
     pair_of = [m0, (m0 + 3 + 2 * odd) % 4, (m0 + 5 - 2 * odd) % 4, (m0 + 2) % 4]
-    apart = (2 * h + c - m0 + 4) % 4
-    my_step = jnp.where(
-        apart == 0, 0, jnp.where(apart == 2, 3, jnp.where(apart == 1, 2 - odd, 1 + odd))
-    )
-
     dest_x = (y + 2 * c) % 4
     ahead = (dest_x - x + 4) % 4
 
@@ -266,17 +277,29 @@
     def reduces(step):
         return active & (c == pair_of[step] % 2)
 
-    def final_remote(step, side):
+    def half_of(step):
+        home = pair_of[step] // 2
+        return (home - h) * (home - h)
+
+    def final_remotes(step, side):
         unit = 2 * step + side
-        home = pair_of[step] // 2
-        here = 1 - (home - h) * (home - h)
-        return remote(
-            reduced.at[unit], reduced.at[9 - here], final_send.at[unit], final_recv.at[1 - here],
-            at_dp(y1 if side else y, z), tensor_of(x, home, c),
-        )
-
-    def stays(step, side):
-        return (pair_of[step] // 2 == h) if side == 0 else False
+        half = half_of(step)
+        same, across = 8 + 2 * half, 11 - 2 * half
+        source = reduced.at[unit if side else same]
+        copies = [
+            remote(
+                source, reduced.at[across], final_send.at[unit, 0], final_recv.at[across - 8],
+                at_dp(y1 if side else y, z), tensor_of(x, 1 - h, c),
+            )
+        ]
+        if side:
+            copies.append(
+                remote(
+                    source, reduced.at[same], final_send.at[unit, 1], final_recv.at[same - 8],
+                    at_dp(y1, z), me,
+                )
+            )
+        return copies
 
     def reduce_x(step, side):
         unit = 2 * step + side
@@ -289,11 +312,7 @@
 
             arrived(from_minus.at[unit], minus_recv.at[unit], x_send.at[unit])
             arrived(from_plus.at[unit], plus_recv.at[unit], x_send.at[unit])
-            if side == 0:
-                home = pair_of[step] // 2
-                target = jnp.where(home == h, 8, unit)
-            else:
-                target = unit
+            target = unit if side else 8 + 2 * half_of(step)
 
             def body(part):
                 reduced[target, part, :] = (
@@ -303,21 +322,15 @@
                 ).astype(BF16)
 
             by_rows(body)
-            if side == 0:
-
-                @pl.when(pair_of[step] // 2 != h)
-                def _():
-                    final_remote(step, side).start()
-
-            else:
-                final_remote(step, side).start()
+            for copy in final_remotes(step, side):
+                copy.start()
 
     def table_copy(half, i):
         spot = ((2 * x + c) + i) % 8
         to = tensor_of(spot // 2, h, spot % 2)
         source = tensor_of(x, (h + half) % 2, c)
         return remote(
-            stage.at[half, i], table_grads.at[source], table_send.at[half, i],
+            stage.at[half, i], table_grads.at[source % 4, source // 4], table_send.at[half, i],
             table_recv.at[source], dp, to,
         )
 
@@ -325,11 +338,11 @@
         source = tensor_of(x, (h + half) % 2, c)
 
         def chosen(owner):
-            table = slots_ref[0, owner]
+            slot = slots_ref[0, owner]
             value = held[half, :, 0:128]
             for number in range(1, 4):
                 columns = held[half, :, 128 * number : 128 * (number + 1)]
-                value = jnp.where(table == number, columns, value)
+                value = jnp.where(slot >= 4 * number, columns, value)
             return value
 
         @pl.loop(1, 8)
@@ -338,136 +351,131 @@
             stage[half, i] = chosen(tensor_of(spot // 2, h, spot % 2))
             table_copy(half, i).start()
 
-        table_grads[source] = chosen(me)
-
-    to_half = remote(
-        held.at[0], held.at[1], half_send.at[0], half_recv.at[0], dp, tensor_of(x, 1 - h, c)
-    )
-    write_pooled = pltpu.make_async_copy(held.at[0], pooled_ref, local_sem.at[6])
-
-    def finish_pooled():
+        table_grads[source % 4, source // 4] = chosen(me)
+
+    write_pooled = pltpu.make_async_copy(held.at[0], pooled_ref, local_sem.at[4])
+
+    def finish(half):
+        here, across = 8 + 2 * half, 9 + 2 * half
+
         @pl.when(jnp.logical_not(active))
         def _():
-            arrived(reduced.at[8], final_recv.at[0], final_send.at[0])
-
-        arrived(reduced.at[9], final_recv.at[1], final_send.at[0])
+            arrived(reduced.at[here], final_recv.at[here - 8], final_send.at[0, 0])
+
+        arrived(reduced.at[across], final_recv.at[across - 8], final_send.at[0, 0])
 
         def body(part):
-            held[0, part, :] = (
-                direct[part, :].astype(F32)
-                + (reduced[8, part, :].astype(F32) + reduced[9, part, :].astype(F32))
+            held[half, part, :] = (
+                direct[half, part, :].astype(F32)
+                + (reduced[here, part, :].astype(F32) + reduced[across, part, :].astype(F32))
             ).astype(BF16)
 
         by_rows(body)
-        to_half.start()
-        write_pooled.start()
-        send_tables(0)
-
-    def finish_other():
-        arrived(held.at[1], half_recv.at[0], half_send.at[0])
-        send_tables(1)
+        if half == 0:
+            write_pooled.start()
+        send_tables(half)
+
+    def finish_step(step):
+        @pl.when(c == pair_of[step] % 2)
+        def _():
+            @pl.when(half_of(step) == 0)
+            def _():
+                finish(0)
+
+            @pl.when(half_of(step) == 1)
+            def _():
+                finish(1)
 
     def scatter(step):
+        block = pair_of[step]
+
         @pl.loop(0, 4)
         def _(xx):
-            source = 4 * xx + pair_of[step]
-
-            @pl.when((xx != x) | (pair_of[step] % 2 != c))
+            source = 4 * xx + block
+
+            @pl.when((xx != x) | (block % 2 != c))
             def _():
-                arrived(table_grads.at[source], table_recv.at[source], table_send.at[0, 1])
-
-            row_grad[...] += jnp.dot(
-                counts[source], table_grads[source], preferred_element_type=F32
-            )
-
-    row_grad[...] = jnp.zeros_like(row_grad)
+                arrived(table_grads.at[block, xx], table_recv.at[source], table_send.at[0, 1])
+
+        part = jnp.dot(
+            counts[block],
+            table_grads[block].reshape(1024, 128),
+            preferred_element_type=F32,
+        )
+        if step == 0:
+            row_grad[...] = part
+        else:
+            row_grad[...] += part
+
+    ring_wait(1, 0)
+    ring_start(2, 0)
+    count(0, 4)
     arrived(place(z, 1), pair_recv.at[0], pair_send.at[0])
     ring_start(1, 1)
-    loads[2].wait()
-    ring_wait(1, 0)
-    ring_start(2, 0)
-    count(0, 3)
+    to_side.start()
+    ring_wait(2, 0)
+    ring_start(3, 0)
+    count(4, 12)
     ring_wait(1, 1)
     ring_start(2, 1)
+    loads[2].wait()
     multiply(0, 0)
-    count(3, 6)
-    ring_wait(2, 0)
-    ring_start(3, 0)
+    count(12, 16)
+    ring_wait(3, 0)
+    ring_start(4, 0)
     combine(0, 0)
-    count(6, 9)
+    loads[3].wait()
     ring_wait(2, 1)
     ring_start(3, 1)
     multiply(1, 0)
     relay_on(0, 0)
-    count(9, 12)
     combine(1, 0)
-    ring_wait(3, 0)
-    ring_start(4, 0)
+    arrived(weights.at[1], pair_recv.at[1], pair_send.at[1])
+    to_other.start()
+    multiply(0, 1)
+    multiply(1, 1)
     reduce_x(0, 0)
+    combine(0, 1)
+    combine(1, 1)
     relay_on(1, 0)
-    count(12, 16)
-    loads[4].wait()
-    loads[5].wait()
     ring_wait(3, 1)
     ring_start(4, 1)
-    arrived(weights.at[1], pair_recv.at[1], pair_send.at[1])
-    multiply(0, 1)
-    multiply(1, 1)
-    combine(0, 1)
     multiply(2, 0)
-    combine(1, 1)
     multiply(2, 1)
     relay_on(0, 1)
+    combine(2, 0)
     relay_on(1, 1)
-    combine(2, 0)
     combine(2, 1)
+    reduce_x(1, 0)
+    reduce_x(0, 1)
+    relay_on(2, 0)
     ring_wait(4, 0)
     ring_wait(4, 1)
     multiply(3, 0)
     multiply(3, 1)
-    relay_on(2, 0)
     relay_on(2, 1)
     combine(3, 0)
     combine(3, 1)
-    reduce_x(1, 0)
-    reduce_x(0, 1)
     reduce_x(1, 1)
+
     relay_on(3, 0)
     reduce_x(2, 0)
     relay_on(3, 1)
     reduce_x(2, 1)
 
-    @pl.when(my_step != 3)
-    def _():
-        finish_pooled()
-
-    @pl.when(my_step != 0)
-    def _():
-        finish_other()
-
     reduce_x(3, 0)
     reduce_x(3, 1)
-
-    @pl.when(my_step == 3)
-    def _():
-        finish_pooled()
-
-    @pl.when(my_step == 0)
-    def _():
-        finish_other()
-
+    arrived(direct.at[1], pair_recv.at[2], pair_send.at[2])
+    finish_step(0)
+    finish_step(1)
+    finish_step(2)
+    finish_step(3)
     scatter(0)
     scatter(1)
     scatter(2)
     scatter(3)
-
-    new_acc = acc_wide[...] + jnp.mean(row_grad[...] * row_grad[...], axis=-1, keepdims=True)
-    rows[...] = rows[...] - learn_rate * row_grad[...] / jnp.sqrt(new_acc)
-    acc_out[...] = new_acc.T[0:1, :]
-    write_rows = pltpu.make_async_copy(rows, new_rows_ref, local_sem.at[7])
-    write_acc = pltpu.make_async_copy(acc_out, new_acc_ref, local_sem.at[8])
+    write_rows = pltpu.make_async_copy(row_grad, row_grad_ref, local_sem.at[5])
     write_rows.start()
-    write_acc.start()
 
     for step in range(1, 5):
         for slot in range(2):
@@ -475,6 +483,7 @@
             ring_down(step, slot).wait_send()
     to_pair.wait_send()
     to_side.wait_send()
+    to_other.wait_send()
 
     @pl.loop(1, 16)
     def _(i):
@@ -489,15 +498,10 @@
             def _():
                 sent(summed.at[0, unit], x_send.at[unit], own_recv.at[unit])
 
-            away = reduces(step)
-            if side == 0:
-                away = away & (pair_of[step] // 2 != h)
-
-            @pl.when(away)
+            @pl.when(reduces(step))
             def _():
-                sent(reduced.at[unit], final_send.at[unit], final_recv.at[0])
-
-    to_half.wait_send()
+                for copy in final_remotes(step, side):
+                    copy.wait_send()
 
     @pl.loop(1, 8)
     def _(i):
@@ -506,7 +510,6 @@
 
     write_pooled.wait()
     write_rows.wait()
-    write_acc.wait()
 
 
 def local(
@@ -514,47 +517,42 @@
 ):
     anywhere = pl.BlockSpec(memory_space=pl.ANY)
     dma = pltpu.SemaphoreType.DMA
-    pooled, new_rows, new_acc = pl.pallas_call(
+    pooled, row_grad = pl.pallas_call(
         kernel,
         out_shape=(
             jax.ShapeDtypeStruct((256, 512), BF16),
             jax.ShapeDtypeStruct((1024, 128), F32),
-            jax.ShapeDtypeStruct((1, 1024), F32),
         ),
         in_specs=[anywhere] * 4
-        + [pl.BlockSpec(memory_space=pltpu.VMEM), pl.BlockSpec(memory_space=pltpu.SMEM)]
-        + [anywhere] * 2,
-        out_specs=(anywhere,) * 3,
+        + [pl.BlockSpec(memory_space=pltpu.VMEM), pl.BlockSpec(memory_space=pltpu.SMEM)],
+        out_specs=(anywhere,) * 2,
         scratch_shapes=[
             pltpu.VMEM((2, 128, 1024), BF16),
             pltpu.VMEM((4, 512, 1024), BF16),
             pltpu.VMEM((2, 1024, 512), BF16),
-            pltpu.VMEM((256, 512), BF16),
-            pltpu.VMEM((1024, 128), F32),
-            pltpu.VMEM((1, 1024), F32),
-            pltpu.VMEM((1024, 128), F32),
+            pltpu.VMEM((2, 256, 512), BF16),
             pltpu.VMEM((8, 2, 256, 512), BF16),
             pltpu.VMEM((8, 256, 512), BF16),
             pltpu.VMEM((2, 8, 256, 512), BF16),
             pltpu.VMEM((8, 256, 512), BF16),
             pltpu.VMEM((8, 256, 512), BF16),
             pltpu.VMEM((8, 256, 512), BF16),
-            pltpu.VMEM((10, 256, 512), BF16),
+            pltpu.VMEM((12, 256, 512), BF16),
             pltpu.VMEM((2, 256, 512), BF16),
             pltpu.VMEM((2, 8, 256, 128), BF16),
-            pltpu.VMEM((16, 256, 128), BF16),
+            pltpu.VMEM((4, 4, 256, 128), BF16),
             pltpu.VMEM((16, 8, 256), jnp.int32),
             pltpu.VMEM((16, 8, 256), jnp.int32),
-            pltpu.VMEM((16, 1024, 256), BF16),
+            pltpu.VMEM((128, 256), jnp.int32),
+            pltpu.VMEM((4, 1024, 1024), BF16),
             pltpu.VMEM((1024, 128), F32),
-            pltpu.VMEM((1, 1024), F32),
-            dma((9,)),
+            dma((6,)),
             dma((4, 2)),
             dma((4, 2)),
             dma((4, 2)),
             dma((4, 2)),
-            dma((2,)),
-            dma((2,)),
+            dma((3,)),
+            dma((3,)),
             dma((8,)),
             dma((8,)),
             dma((8,)),
@@ -562,10 +560,8 @@
             dma((8,)),
             dma((8,)),
             dma((8,)),
-            dma((8,)),
-            dma((2,)),
-            dma((1,)),
-            dma((1,)),
+            dma((8, 2)),
+            dma((4,)),
             dma((2, 8)),
             dma((16,)),
             dma((16,)),
@@ -583,11 +579,11 @@
         cross_weight,
         direct_grad,
         jnp.transpose(bag_ids, (1, 2, 0)),
-        jnp.concatenate([unit_slots // 4, unit_slots % 4 * 1024]),
-        table_rows[0, 0],
-        adagrad_acc[0],
+        unit_slots,
     )
-    return (pooled, new_rows[None, None], new_acc[None])
+    new_acc = adagrad_acc[0, 0] + jnp.mean(row_grad * row_grad, axis=-1)
+    new_rows = table_rows[0, 0] - learn_rate * row_grad / jnp.sqrt(new_acc)[:, None]
+    return (pooled, new_rows[None, None], new_acc[None, None])
 
 
 def solution(mesh):

time: 143 us -> 118 us (0.83)
  the two profiles are of different devices: /device:TPU:73 before, /device:TPU:1 now
where the time goes in v2:
time: 118 us
  Pallas kernels  114 us (97%)
  other arithmetic  2.92 us (2%)
    pallas_call x1, Pallas kernels, local(): pl.pallas_call(kernel, out_shape=(jax.ShapeDtypeStruct((256, 512), BF16),...  114 us

profile of v2, /device:TPU:1, one launch (start us, length us, event | category | flops | bytes accessed | tf_op | source)
XLA Modules:
  0.0 118.1 jit_solution(14623973082181792165)
XLA Ops:
  0.6 0.0 copy-start.1
  0.6 113.8 %shard_map.103 = (bf16[256,512]{1,0:T(8,128)(2,1)}, f32[1024,128]{1,0:T(8,128)}) custom-call(bf16[128,1024]{1,0:T(8,128)(2,1)} %emb_ref.1, bf16[128,1024]{1,0:T(8,128)(2,1)} %cross_ref.1, bf16[1024,512]{1,0:T(8,128)(2,1)} %weight_ref.1, bf16[256,512]{1,0:T(8,128)(2,1)} %direct_ref.1, s32[4,8,256]{2,1,0:T(8,128)} %bitcast.11, s32[1,16]{1,0:T(1,128)} %slots_ref.1), custom_call_target="tpu_custom_call" | custom-call | flops 5400000000 | bytes 4000000 | tf_op jit(solution)/shard_map/pallas_call | solution.py:520
  114.4 0.0 copy-start
  114.4 0.0 copy-start.3
  114.4 1.3 %multiply_reduce_fusion = f32[1024]{0:T(1024)S(1)} fusion(f32[1024,128]{1,0:T(8,128)} %get-tuple-element.6), kind=kLoop, calls=%fused_computation.2 | loop fusion | flops 261120 | bytes 528384 | tf_op jit(solution)/shard_map/reduce_sum | solution.py:584
  115.8 0.0 copy-done.3
  115.8 0.6 add.11
  116.4 0.0 copy-done.1
  116.4 0.0 copy-done
  116.4 0.0 copy-start.2
  116.4 1.0 fusion
  117.4 0.0 copy-done.2
  117.4 0.7 copy.12
  (1 shorter events, 0.0 us)
Async XLA Ops:
  0.6 115.7 %copy-start.1 = (f32[1,1,1024,128]{3,2,1,0:T(8,128)S(1)}, f32[1,1,1024,128]{3,2,1,0:T(8,128)}, u32[]{:S(2)}) copy-start(f32[1,1,1024,128]{3,2,1,0:T(8,128)} %param.14) | copy-start | bytes 1572868
  114.4 2.0 %copy-start = (f32[1024,128]{1,0:T(8,128)S(1)}, f32[1024,128]{1,0:T(8,128)}, u32[]{:S(2)}) copy-start(f32[1024,128]{1,0:T(8,128)} %get-tuple-element.6) | copy-start | bytes 1572868
  114.4 1.3 %copy-start.3 = (f32[1,1,1024]{2,1,0:T(1,128)S(1)}, f32[1,1,1024]{2,1,0:T(1,128)}, u32[]{:S(2)}) copy-start(f32[1,1,1024]{2,1,0:T(1,128)} %param.15) | copy-start | bytes 12292
  116.4 1.0 copy-start.2

commit v3 on v2

--- a/solution.py
+++ b/solution.py
@@ -409,10 +409,10 @@
 
     ring_wait(1, 0)
     ring_start(2, 0)
+    to_side.start()
     count(0, 4)
     arrived(place(z, 1), pair_recv.at[0], pair_send.at[0])
     ring_start(1, 1)
-    to_side.start()
     ring_wait(2, 0)
     ring_start(3, 0)
     count(4, 12)
@@ -447,22 +447,20 @@
     relay_on(1, 1)
     combine(2, 1)
     reduce_x(1, 0)
-    reduce_x(0, 1)
-    relay_on(2, 0)
     ring_wait(4, 0)
     ring_wait(4, 1)
     multiply(3, 0)
     multiply(3, 1)
-    relay_on(2, 1)
     combine(3, 0)
     combine(3, 1)
+    reduce_x(0, 1)
+    relay_on(2, 0)
+    relay_on(2, 1)
     reduce_x(1, 1)
-
     relay_on(3, 0)
     reduce_x(2, 0)
     relay_on(3, 1)
     reduce_x(2, 1)
-
     reduce_x(3, 0)
     reduce_x(3, 1)
     arrived(direct.at[1], pair_recv.at[2], pair_send.at[2])

time: 118 us -> 116 us (0.983)
  Pallas kernels: 114 us -> 111 us
    pallas_call x1, Pallas kernels: 114 us -> 111 us  [local(): pl.pallas_call(kernel, out_shape=(jax.ShapeDtypeStruct((256, 512), BF16),...]
where the time goes in v3:
time: 116 us; the launch traced here: 115 us
  Pallas kernels  111 us (96%)
  other arithmetic  2.92 us (3%)
    pallas_call x1, Pallas kernels, local(): pl.pallas_call(kernel, out_shape=(jax.ShapeDtypeStruct((256, 512), BF16),...  111 us

profile of v3, /device:TPU:1, one launch (start us, length us, event | category | flops | bytes accessed | tf_op | source)
XLA Modules:
  0.0 115.5 jit_solution(10664698625017317609)
XLA Ops:
  0.6 0.0 copy-start.1
  0.6 111.1 %shard_map.103 = (bf16[256,512]{1,0:T(8,128)(2,1)}, f32[1024,128]{1,0:T(8,128)}) custom-call(bf16[128,1024]{1,0:T(8,128)(2,1)} %emb_ref.1, bf16[128,1024]{1,0:T(8,128)(2,1)} %cross_ref.1, bf16[1024,512]{1,0:T(8,128)(2,1)} %weight_ref.1, bf16[256,512]{1,0:T(8,128)(2,1)} %direct_ref.1, s32[4,8,256]{2,1,0:T(8,128)} %bitcast.11, s32[1,16]{1,0:T(1,128)} %slots_ref.1), custom_call_target="tpu_custom_call" | custom-call | flops 5400000000 | bytes 4000000 | tf_op jit(solution)/shard_map/pallas_call | solution.py:518
  111.8 0.0 copy-start
  111.8 0.0 copy-start.3
  111.8 1.3 %multiply_reduce_fusion = f32[1024]{0:T(1024)S(1)} fusion(f32[1024,128]{1,0:T(8,128)} %get-tuple-element.6), kind=kLoop, calls=%fused_computation.2 | loop fusion | flops 261120 | bytes 528384 | tf_op jit(solution)/shard_map/reduce_sum | solution.py:582
  113.1 0.0 copy-done.3
  113.2 0.6 add.11
  113.8 0.0 copy-done.1
  113.8 0.0 copy-done
  113.8 0.0 copy-start.2
  113.8 1.0 fusion
  114.8 0.0 copy-done.2
  114.8 0.7 copy.12
  (1 shorter events, 0.0 us)
Async XLA Ops:
  0.6 113.1 %copy-start.1 = (f32[1,1,1024,128]{3,2,1,0:T(8,128)S(1)}, f32[1,1,1024,128]{3,2,1,0:T(8,128)}, u32[]{:S(2)}) copy-start(f32[1,1,1024,128]{3,2,1,0:T(8,128)} %param.14) | copy-start | bytes 1572868
  111.8 2.0 %copy-start = (f32[1024,128]{1,0:T(8,128)S(1)}, f32[1024,128]{1,0:T(8,128)}, u32[]{:S(2)}) copy-start(f32[1024,128]{1,0:T(8,128)} %get-tuple-element.6) | copy-start | bytes 1572868
  111.8 1.3 %copy-start.3 = (f32[1,1,1024]{2,1,0:T(1,128)S(1)}, f32[1,1,1024]{2,1,0:T(1,128)}, u32[]{:S(2)}) copy-start(f32[1,1,1024]{2,1,0:T(1,128)} %param.15) | copy-start | bytes 12292
  113.8 1.0 copy-start.2

commit v4 on v3

--- a/solution.py
+++ b/solution.py
@@ -85,36 +85,61 @@
 
     pl.semaphore_wait(barrier, 20)
 
-    def ring_up(step, slot):
-        origin = (z + 9 - step) % 8
-        ref = place(origin, slot, 0, 64 if step == 4 else 128)
+    def ring_up(step, slot, part):
+        ref = place((z + 9 - step) % 8, slot, 64 * part, 64)
         return remote(
-            ref, ref, up_send.at[step - 1, slot], up_recv.at[step - 1, slot], at_dp(y, up), me
-        )
-
-    def ring_down(step, slot):
-        origin = (z + step - 1) % 8
-        ref = place(origin, slot, 64, 64) if step == 4 else place(origin, slot)
+            ref, ref, up_send.at[step - 1, slot, part], up_recv.at[step - 1, slot, part],
+            at_dp(y, up), me,
+        )
+
+    def ring_down(step, slot, part):
+        ref = place((z + step - 1) % 8, slot, 64 * part, 64)
         return remote(
-            ref, ref, down_send.at[step - 1, slot], down_recv.at[step - 1, slot], at_dp(y, down), me
-        )
-
-    def ring_start(step, slot):
-        ring_up(step, slot).start()
-        ring_down(step, slot).start()
-
-    def ring_wait(step, slot):
-        low = place((z + 8 - step) % 8, slot, 0, 64 if step == 4 else 128)
-        arrived(low, up_recv.at[step - 1, slot], up_send.at[step - 1, slot])
-        high_origin = (z + step) % 8
-        high = place(high_origin, slot, 64, 64) if step == 4 else place(high_origin, slot)
-        arrived(high, down_recv.at[step - 1, slot], down_send.at[step - 1, slot])
+            ref, ref, down_send.at[step - 1, slot, part], down_recv.at[step - 1, slot, part],
+            at_dp(y, down), me,
+        )
+
+    def ring_copies(step, slot, part):
+        copies = []
+        if step < 4 or part == 0:
+            copies.append(ring_up(step, slot, part))
+        if step < 4 or part == 1:
+            copies.append(ring_down(step, slot, part))
+        return copies
+
+    def ring_start(step, slot, parts=(0, 1)):
+        for part in parts:
+            for copy in ring_copies(step, slot, part):
+                copy.start()
+
+    def ring_wait(step, slot, parts=(0, 1)):
+        for part in parts:
+            if step < 4 or part == 0:
+                arrived(
+                    place((z + 8 - step) % 8, slot, 64 * part, 64),
+                    up_recv.at[step - 1, slot, part], up_send.at[step - 1, slot, part],
+                )
+            if step < 4 or part == 1:
+                arrived(
+                    place((z + step) % 8, slot, 64 * part, 64),
+                    down_recv.at[step - 1, slot, part], down_send.at[step - 1, slot, part],
+                )
+
+    def ring_pass(step, slot):
+        for part in (0, 1):
+            ring_wait(step, slot, (part,))
+            ring_start(step + 1, slot, (part,))
 
     ring_start(1, 0)
-    to_pair = remote(
-        own, place(z, 1), pair_send.at[0], pair_recv.at[0], at_dp(y2, z), me
-    )
-    to_pair.start()
+    to_pair = [
+        remote(
+            place(z, 0, 64 * part, 64), place(z, 1, 64 * part, 64), pair_send.at[3 * part],
+            pair_recv.at[3 * part], at_dp(y2, z), me,
+        )
+        for part in range(2)
+    ]
+    for copy in to_pair:
+        copy.start()
     to_side = remote(
         weight_ref, weights.at[1], pair_send.at[1], pair_recv.at[1], at_dp(y1, z), me
     )
@@ -407,26 +432,22 @@
         else:
             row_grad[...] += part
 
-    ring_wait(1, 0)
-    ring_start(2, 0)
     to_side.start()
+    ring_pass(1, 0)
     count(0, 4)
-    arrived(place(z, 1), pair_recv.at[0], pair_send.at[0])
-    ring_start(1, 1)
-    ring_wait(2, 0)
-    ring_start(3, 0)
+    for part in range(2):
+        arrived(place(z, 1, 64 * part, 64), pair_recv.at[3 * part], pair_send.at[3 * part])
+        ring_start(1, 1, (part,))
+    ring_pass(2, 0)
     count(4, 12)
-    ring_wait(1, 1)
-    ring_start(2, 1)
+    ring_pass(1, 1)
     loads[2].wait()
     multiply(0, 0)
     count(12, 16)
-    ring_wait(3, 0)
-    ring_start(4, 0)
+    ring_pass(3, 0)
     combine(0, 0)
     loads[3].wait()
-    ring_wait(2, 1)
-    ring_start(3, 1)
+    ring_pass(2, 1)
     multiply(1, 0)
     relay_on(0, 0)
     combine(1, 0)
@@ -438,8 +459,7 @@
     combine(0, 1)
     combine(1, 1)
     relay_on(1, 0)
-    ring_wait(3, 1)
-    ring_start(4, 1)
+    ring_pass(3, 1)
     multiply(2, 0)
     multiply(2, 1)
     relay_on(0, 1)
@@ -451,24 +471,24 @@
     ring_wait(4, 1)
     multiply(3, 0)
     multiply(3, 1)
+    relay_on(2, 0)
     combine(3, 0)
+    relay_on(2, 1)
     combine(3, 1)
     reduce_x(0, 1)
-    relay_on(2, 0)
-    relay_on(2, 1)
     reduce_x(1, 1)
     relay_on(3, 0)
     reduce_x(2, 0)
     relay_on(3, 1)
     reduce_x(2, 1)
-    reduce_x(3, 0)
-    reduce_x(3, 1)
     arrived(direct.at[1], pair_recv.at[2], pair_send.at[2])
     finish_step(0)
     finish_step(1)
+    reduce_x(3, 0)
+    reduce_x(3, 1)
+    scatter(0)
     finish_step(2)
     finish_step(3)
-    scatter(0)
     scatter(1)
     scatter(2)
     scatter(3)
@@ -477,9 +497,11 @@
 
     for step in range(1, 5):
         for slot in range(2):
-            ring_up(step, slot).wait_send()
-            ring_down(step, slot).wait_send()
-    to_pair.wait_send()
+            for part in range(2):
+                for copy in ring_copies(step, slot, part):
+                    copy.wait_send()
+    for copy in to_pair:
+        copy.wait_send()
     to_side.wait_send()
     to_other.wait_send()
 
@@ -545,12 +567,12 @@
             pltpu.VMEM((4, 1024, 1024), BF16),
             pltpu.VMEM((1024, 128), F32),
             dma((6,)),
-            dma((4, 2)),
-            dma((4, 2)),
-            dma((4, 2)),
-            dma((4, 2)),
-            dma((3,)),
-            dma((3,)),
+            dma((4, 2, 2)),
+            dma((4, 2, 2)),
+            dma((4, 2, 2)),
+            dma((4, 2, 2)),
+            dma((4,)),
+            dma((4,)),
             dma((8,)),
             dma((8,)),
             dma((8,)),

time: 116 us -> 114 us (0.983)
    pallas_call x1, Pallas kernels: 111 us -> 110 us  [local(): pl.pallas_call(kernel, out_shape=(jax.ShapeDtypeStruct((256, 512), BF16),...]
where the time goes in v4:
time: 114 us
  Pallas kernels  110 us (96%)
  other arithmetic  2.92 us (3%)
    pallas_call x1, Pallas kernels, local(): pl.pallas_call(kernel, out_shape=(jax.ShapeDtypeStruct((256, 512), BF16),...  110 us

profile of v4, /device:TPU:1, one launch (start us, length us, event | category | flops | bytes accessed | tf_op | source)
XLA Modules:
  0.0 114.2 jit_solution(11012016015611312868)
XLA Ops:
  0.6 0.0 copy-start.1
  0.6 109.8 %shard_map.103 = (bf16[256,512]{1,0:T(8,128)(2,1)}, f32[1024,128]{1,0:T(8,128)}) custom-call(bf16[128,1024]{1,0:T(8,128)(2,1)} %emb_ref.1, bf16[128,1024]{1,0:T(8,128)(2,1)} %cross_ref.1, bf16[1024,512]{1,0:T(8,128)(2,1)} %weight_ref.1, bf16[256,512]{1,0:T(8,128)(2,1)} %direct_ref.1, s32[4,8,256]{2,1,0:T(8,128)} %bitcast.11, s32[1,16]{1,0:T(1,128)} %slots_ref.1), custom_call_target="tpu_custom_call" | custom-call | flops 5400000000 | bytes 4000000 | tf_op jit(solution)/shard_map/pallas_call | solution.py:540
  110.5 0.0 copy-start
  110.5 0.0 copy-start.3
  110.5 1.3 %multiply_reduce_fusion = f32[1024]{0:T(1024)S(1)} fusion(f32[1024,128]{1,0:T(8,128)} %get-tuple-element.6), kind=kLoop, calls=%fused_computation.2 | loop fusion | flops 261120 | bytes 528384 | tf_op jit(solution)/shard_map/reduce_sum | solution.py:604
  111.8 0.0 copy-done.3
  111.8 0.6 add.11
  112.4 0.0 copy-done.1
  112.4 0.0 copy-done
  112.5 0.0 copy-start.2
  112.5 1.0 fusion
  113.5 0.0 copy-done.2
  113.5 0.7 copy.12
  (1 shorter events, 0.0 us)
Async XLA Ops:
  0.6 111.8 %copy-start.1 = (f32[1,1,1024,128]{3,2,1,0:T(8,128)S(1)}, f32[1,1,1024,128]{3,2,1,0:T(8,128)}, u32[]{:S(2)}) copy-start(f32[1,1,1024,128]{3,2,1,0:T(8,128)} %param.14) | copy-start | bytes 1572868
  110.5 2.0 %copy-start = (f32[1024,128]{1,0:T(8,128)S(1)}, f32[1024,128]{1,0:T(8,128)}, u32[]{:S(2)}) copy-start(f32[1024,128]{1,0:T(8,128)} %get-tuple-element.6) | copy-start | bytes 1572868
  110.5 1.3 %copy-start.3 = (f32[1,1,1024]{2,1,0:T(1,128)S(1)}, f32[1,1,1024]{2,1,0:T(1,128)}, u32[]{:S(2)}) copy-start(f32[1,1,1024]{2,1,0:T(1,128)} %param.15) | copy-start | bytes 12292
  112.5 1.0 copy-start.2
